TPU v7x, 512 devices: a whole 4x8x8 slice. The times are simulated.
512 devices in a mesh: section: 64 (over y, z), rep: 8 (over x, core).
Axes of the slice: x: 4, y: 8, z: 8, core: 2. Of those that a mesh axis runs over, the one named last changes fastest.
Arguments:
- node_features: bfloat16 [65536, 256], P(('section', 'rep')), may hold values from -6 to 6
- tile_values: bfloat16 [8192, 128, 128], P(('section', 'rep')), may hold values from -0.5 to 0.5
- tile_rows: int32 [8192], P(('section', 'rep')), may hold values from 0 to 7
- tile_cols: int32 [8192], P(('section', 'rep')), may hold values from 0 to 63
- tile_counts: int32 [512], P(('section', 'rep')), may hold values from 1 to 16, as said below
- cheb_weights: bfloat16 [768, 256], replicated, may hold values from -0.21875 to 0.21875
- bias: float32 [256], replicated, may hold values from -3 to 3
- out_cotangent: bfloat16 [65536, 256], P(('section', 'rep')), may hold values from -0.0625 to 0.0625
Outputs:
- layer_out: bfloat16 [65536, 256], P(('section', 'rep'))
- weight_grads: float32 [768, 256], replicated
Inputs may be any that keep to these rules, and one draw needn't show every extreme that they name: `tile_counts`: some device holds exactly 16 live tiles; the busiest devices hold about twice the mean.
All inputs are finite; a program needn't handle non-finite values.
Results may differ from a plain program's by a relative error of at most 0.0067.
Values may be sent and summed in bfloat16 or wider, within the bound.
A program may use at most 64 MiB of HBM per device.

v0:
```python
import jax
import jax.numpy as jnp
from jax import lax
from jax.sharding import PartitionSpec as P


def smooth_gate(values):
    return jax.nn.gelu(values, approximate=True)


def propagate(features, tile_values, tile_rows, tile_cols, tile_counts):
    block = tile_values.shape[1]
    width = features.shape[1]
    local_blocks = features.shape[0] // block
    section_blocks = local_blocks * lax.axis_size("rep")
    gathered = lax.all_gather(features, "section", axis=0, tiled=True)
    picked = gathered.reshape(-1, block, width)[tile_cols]
    products = jnp.einsum("tij,tjf->tif", tile_values, picked, preferred_element_type=jnp.float32)
    live = jnp.arange(tile_rows.shape[0], dtype=jnp.int32) < tile_counts[0]
    targets = jnp.arange(section_blocks, dtype=jnp.int32)
    summed = jnp.einsum(
        "bt,tif->bif",
        ((tile_rows[None, :] == targets[:, None]) & live[None, :]).astype(jnp.float32),
        products,
        precision=lax.Precision.HIGHEST,
    )
    return lax.psum_scatter(
        summed.reshape(section_blocks * block, width), "rep", scatter_dimension=0, tiled=True
    )


def body(
    node_features, tile_values, tile_rows, tile_cols, tile_counts, cheb_weights, bias, out_cotangent
):
    first_sum = propagate(node_features, tile_values, tile_rows, tile_cols, tile_counts)
    first_hop = first_sum.astype(jnp.bfloat16)
    second_sum = propagate(first_hop, tile_values, tile_rows, tile_cols, tile_counts)
    second_hop = (2.0 * second_sum - node_features.astype(jnp.float32)).astype(jnp.bfloat16)
    stacked = jnp.concatenate([node_features, first_hop, second_hop], axis=1)
    pre_act = jnp.dot(stacked, cheb_weights, preferred_element_type=jnp.float32) + bias
    layer_out, backward = jax.vjp(smooth_gate, pre_act)
    pre_grad = backward(out_cotangent.astype(jnp.float32))[0].astype(jnp.bfloat16)
    local_grads = jnp.einsum("nk,nf->kf", stacked, pre_grad, preferred_element_type=jnp.float32)
    weight_grads = lax.psum(local_grads, ("section", "rep"))
    return (layer_out.astype(jnp.bfloat16), weight_grads)


def solution(mesh):
    return jax.shard_map(
        body,
        mesh=mesh,
        in_specs=(
            P(("section", "rep"), None),
            P(("section", "rep"), None, None),
            P(("section", "rep")),
            P(("section", "rep")),
            P(("section", "rep")),
            P(),
            P(),
            P(("section", "rep"), None),
        ),
        out_specs=(P(("section", "rep"), None), P()),
        check_vma=False,
    )
```

profile of v0, /device:TPU:1, one launch (start us, length us, event | category | flops | bytes accessed | tf_op | source)
XLA Modules:
  0.0 568.6 jit_solution(1728461831021868884)
XLA Ops:
  7.2 0.0 copy-start
  7.2 0.0 all-gather.3.cloned.1.call-start
  7.2 0.7 all-gather.3.cloned.1.call-update
  7.9 0.0 reduce-scatter.3.cloned.1.call-start
  8.6 0.7 compare_select_fusion
  9.3 90.5 %all-gather.3.cloned.1.call-done = bf16[8192,256]{1,0:T(8,128)(2,1)} async-done(((bf16[128,256]{1,0:T(8,128)(2,1)}), bf16[8192,256]{1,0:T(8,128)(2,1)}) %all-gather.3.cloned.1.call-update) | async-done | bytes 4194320 | tf_op jit(solution)/shard_map/all_gather | solution.py:16
  99.8 3.8 gather_fusion
  103.6 1.7 fusion.38
  105.3 2.1 copy.12
  107.4 2.4 fusion.2
  109.8 1.3 copy.10
  111.1 0.0 reduce-scatter.3.cloned.1.call-update
  111.1 0.0 all-gather.5.cloned.1.call-start
  111.1 36.2 %reduce-scatter.3.cloned.1.call-done = f32[128,256]{1,0:T(8,128)} async-done(((f32[1024,256]{1,0:T(8,128)}), f32[128,256]{1,0:T(8,128)}) %reduce-scatter.3.cloned.1.call-update) | async-done | bytes 131088 | tf_op jit(solution)/shard_map/reduce_scatter | solution.py:27
  147.3 1.5 convert_element_type.20
  148.9 0.0 all-gather.5.cloned.1.call-update
  148.9 0.0 reduce-scatter.5.cloned.1.call-start
  148.9 85.9 %all-gather.5.cloned.1.call-done = bf16[8192,256]{1,0:T(8,128)(2,1)} async-done(((bf16[128,256]{1,0:T(8,128)(2,1)}), bf16[8192,256]{1,0:T(8,128)(2,1)}) %all-gather.5.cloned.1.call-update) | async-done | bytes 4194320 | tf_op jit(solution)/shard_map/all_gather | solution.py:16
  234.8 3.8 gather_fusion.1
  238.6 1.7 fusion.39
  240.3 2.1 copy.13
  242.4 2.4 fusion
  244.8 1.3 copy.11
  246.2 0.0 reduce-scatter.5.cloned.1.call-update
  246.2 0.0 all-reduce.2.cloned.1.call-start
  246.2 36.2 %reduce-scatter.5.cloned.1.call-done = f32[128,256]{1,0:T(8,128)} async-done(((f32[1024,256]{1,0:T(8,128)}), f32[128,256]{1,0:T(8,128)}) %reduce-scatter.5.cloned.1.call-update) | async-done | bytes 131088 | tf_op jit(solution)/shard_map/reduce_scatter | solution.py:27
  282.4 0.9 subtract_convert_fusion
  283.4 0.9 multiply_convert_fusion
  284.2 1.2 fusion.14
  285.5 0.0 all-reduce.2.cloned.1.call-update
  285.5 274.5 %all-reduce.2.cloned.1.call-done = f32[768,256]{1,0:T(8,128)} async-done(((f32[768,256]{1,0:T(8,128)}), f32[768,256]{1,0:T(8,128)}) %all-reduce.2.cloned.1.call-update) | async-done | bytes 786448 | tf_op jit(solution)/shard_map/psum | solution.py:44
  560.0 2.1 copy.16
  (15 shorter events, 0.1 us)
Async XLA Ops:
  7.2 96.4 %copy-start = (bf16[16,128,128]{2,1,0:T(8,128)(2,1)S(1)}, bf16[16,128,128]{2,1,0:T(8,128)(2,1)}, u32[]{:S(2)}) copy-start(bf16[16,128,128]{2,1,0:T(8,128)(2,1)} %param.9) | copy-start | bytes 1572868
  7.2 92.6 %all-gather.3.cloned.1.call-start = ((), (), s32[]{:S(2)}) async-start(), calls=%async_computation.2 | async-start | bytes 4259840 | tf_op jit(solution)/shard_map/all_gather | solution.py:16
  7.9 139.4 %reduce-scatter.3.cloned.1.call-start = ((), (), s32[]{:S(2)}) async-start(), calls=%async_computation.3 | async-start | bytes 1179648 | tf_op jit(solution)/shard_map/reduce_scatter | solution.py:27
  105.3 2.1 copy-start.3
  111.1 123.7 %all-gather.5.cloned.1.call-start = ((), (), s32[]{:S(2)}) async-start(), calls=%async_computation.4 | async-start | bytes 4259840 | tf_op jit(solution)/shard_map/all_gather | solution.py:16
  148.9 133.5 %reduce-scatter.5.cloned.1.call-start = ((), (), s32[]{:S(2)}) async-start(), calls=%async_computation.5 | async-start | bytes 1179648 | tf_op jit(solution)/shard_map/reduce_scatter | solution.py:27
  244.8 37.6 %copy-start.2 = (bf16[128,256]{1,0:T(8,128)(2,1)S(1)}, bf16[128,256]{1,0:T(8,128)(2,1)}, u32[]{:S(2)}) copy-start(bf16[128,256]{1,0:T(8,128)(2,1)} %param.8) | copy-start | bytes 196612
  244.8 38.5 %copy-start.1 = (bf16[128,256]{1,0:T(8,128)(2,1)S(1)}, bf16[128,256]{1,0:T(8,128)(2,1)}, u32[]{:S(2)}) copy-start(bf16[128,256]{1,0:T(8,128)(2,1)} %convert_element_type.20) | copy-start | bytes 196612
  244.8 38.5 %copy-start.4 = (bf16[768,256]{1,0:T(8,128)(2,1)S(1)}, bf16[768,256]{1,0:T(8,128)(2,1)}, u32[]{:S(2)}) copy-start(bf16[768,256]{1,0:T(8,128)(2,1)} %param.13) | copy-start | bytes 1179652
  244.8 38.5 %copy-start.6 = (f32[256]{0:T(256)S(1)}, f32[256]{0:T(256)}, u32[]{:S(2)}) copy-start(f32[256]{0:T(256)} %param.14) | copy-start | bytes 3076
  244.8 39.4 %copy-start.5 = (bf16[128,256]{1,0:T(8,128)(2,1)S(1)}, bf16[128,256]{1,0:T(8,128)(2,1)}, u32[]{:S(2)}) copy-start(bf16[128,256]{1,0:T(8,128)(2,1)} %param.15) | copy-start | bytes 196612
  246.2 313.8 %all-reduce.2.cloned.1.call-start = ((), (), s32[]{:S(2)}) async-start(), calls=%async_computation.6 | async-start | bytes 1572864 | tf_op jit(solution)/shard_map/psum | solution.py:44
Sparse Core Ops, SparseCore 0:
  11.0 88.7 all-gather.2
  111.2 36.0 reduce-scatter.2
  150.9 83.8 all-gather.4
  246.3 36.0 reduce-scatter.4
  287.8 272.1 all-reduce.1
where the time goes:
time: 569 us
  waiting for transfers between devices  524 us (92%)
  local copies, waits for them, and re-layouts  16.4 us (3%)
  between operations  14.5 us (3%)
  matrix products  10.3 us (2%)
    psum x1, waiting for transfers between devices, body(): weight_grads = lax.psum(local_grads, ('section', 'rep'))  274 us
    all_gather x2, waiting for transfers between devices, propagate(): gathered = lax.all_gather(features, 'section', axis=0, tiled=True)  176 us
    reduce_scatter x2, waiting for transfers between devices, propagate(): lax.psum_scatter(summed.reshape(section_blocks * block, width), 'rep', sc...  72.3 us
  transfers between devices with their start and end apart: 5, of which 5 were waited for; matrix products, arithmetic and copies ran while one was open for 0% of the time, Pallas kernels for 0%

commit v1 on v0

v1 whole, which is shorter than its diff:
```python
import jax
import jax.numpy as jnp
from jax import lax
from jax.experimental import pallas as pl
from jax.experimental.pallas import tpu as pltpu
from jax.sharding import PartitionSpec as P

MESH = pl.DeviceIdType.MESH
N = 8
BLOCK = 128
F = 256
HALF = 128
TCAP = 16
BF16 = jnp.bfloat16
F32 = jnp.float32


def kernel(
    rows_ref, cols_ref, count_ref, x_ref, tiles_ref, w_ref, bias_ref, cot_ref,
    out_ref, grad_ref,
    *scratch,
):
    gathers_a, gathers_b = scratch[0:4], scratch[4:8]
    partials, arrivals = scratch[8:12], scratch[12:16]
    (adj, picked, hop1, hop2, grad_send, grad_recv, y_send, y_recv, z_all, y_all, rep_all,
     ring1_send, ring1_recv, ring2_send, ring2_recv, sum_send, sum_recv, red_send, red_recv) = scratch[16:]

    section = lax.axis_index("section")
    rep = lax.axis_index("rep")
    y = section // N
    z = section % N

    def ahead(pos, step):
        return lax.rem(pos + (step % N), N)

    def at_yz(yy, zz):
        return (yy * N + zz, rep)

    barrier = pltpu.get_barrier_semaphore()
    for d in range(1, N):
        for target in (at_yz(ahead(y, d), z), at_yz(y, ahead(z, d)), (section, ahead(rep, d))):
            pl.semaphore_signal(barrier, inc=1, device_id=target, device_id_type=MESH)
    pl.semaphore_wait(barrier, 3 * (N - 1))

    sends = []

    def remote(src, dst, send_sem, recv_sem, target):
        copy = pltpu.make_async_remote_copy(
            src_ref=src, dst_ref=dst, send_sem=send_sem, recv_sem=recv_sem,
            device_id=target, device_id_type=MESH,
        )
        copy.start()
        sends.append(copy)
        return copy

    orders = (
        (gathers_a, y, z, lambda u, v: at_yz(u, v)),
        (gathers_b, z, y, lambda u, v: at_yz(v, u)),
    )
    ring1, ring2 = {}, {}

    def ring1_put(stage, k):
        for o, (bufs, u, v, dev) in enumerate(orders):
            for way in (0, 1):
                if k > 3 + ((way + o + 1) % 2):
                    continue
                sign = 1 if way == 0 else -1
                piece = bufs[stage].at[u, ahead(v, -sign * (k - 1))]
                i = (stage, o, way, k - 1)
                ring1[i] = remote(piece, piece, ring1_send.at[i], ring1_recv.at[i], dev(u, ahead(v, sign)))

    def ring1_take(stage, k):
        for o in (0, 1):
            for way in (0, 1):
                if (stage, o, way, k - 1) in ring1:
                    ring1[stage, o, way, k - 1].wait_recv()

    def ring1_begin(stage, half):
        gathers_a[stage][y, z] = half[:64]
        gathers_b[stage][z, y] = half[64:]
        ring1_put(stage, 1)

    def ring1_step(stage, k):
        ring1_take(stage, k - 1)
        ring1_put(stage, k)

    def ring2_put(stage, k, o, way, sub):
        bufs, u, v, dev = orders[o]
        if k == 4 and sub != way:
            return
        sign = 1 if way == 0 else -1
        group = bufs[stage].at[ahead(u, -sign * (k - 1)), pl.ds(4 * sub, 4)]
        i = (stage, o, way, 2 * (k - 1) + sub)
        ring2[i] = remote(group, group, ring2_send.at[i], ring2_recv.at[i], dev(ahead(u, sign), v))

    def ring2_step(stage, k):
        for sub in (0, 1):
            for o in (0, 1):
                for way in (0, 1):
                    i = (stage, o, way, 2 * (k - 2) + sub)
                    if i in ring2:
                        ring2[i].wait_recv()
                    if k <= 4:
                        ring2_put(stage, k, o, way, sub)

    def ring2_begin(stage):
        ring2_step(stage, 1)

    def place_tiles():
        def one(t, _):
            tile = tiles_ref[t]
            row = jnp.where(t < count_ref[0], rows_ref[t], N)
            for b in range(N):
                adj[b * BLOCK:(b + 1) * BLOCK, pl.ds(pl.multiple_of(t * BLOCK, BLOCK), BLOCK)] = jnp.where(
                    row == b, tile, jnp.zeros_like(tile))
            return 0
        lax.fori_loop(0, TCAP, one, 0)

    sums = {}

    def multiply(stage):
        ga, gb = gathers_a[stage], gathers_b[stage]

        def pick(t, _):
            col = cols_ref[t]
            cy, cz = lax.div(col, N), lax.rem(col, N)
            at = pl.multiple_of(t * BLOCK, BLOCK)
            picked[pl.ds(at, 64), :] = ga[cy, cz]
            picked[pl.ds(at + 64, 64), :] = gb[cz, cy]
            return 0
        lax.fori_loop(0, TCAP, pick, 0)

        def rows(i, _):
            product = jnp.dot(adj[pl.ds(pl.multiple_of(i * 256, 256), 256), :], picked[...], preferred_element_type=F32)
            partials[stage][2 * i] = product[:BLOCK].astype(BF16)
            partials[stage][2 * i + 1] = product[BLOCK:].astype(BF16)
            return 0
        lax.fori_loop(0, N // 2, rows, 0)
        for d in range(1, N):
            to = ahead(rep, d)
            sums[stage, d] = remote(partials[stage].at[to], arrivals[stage].at[d - 1],
                                    sum_send.at[stage, d - 1], sum_recv.at[stage, d - 1], (section, to))

    def total(stage):
        for d in range(1, N):
            sums[stage, d].wait_recv()
        acc = partials[stage][rep].astype(F32)
        for d in range(1, N):
            acc += arrivals[stage][d - 1].astype(F32)
        return acc

    def first_total(c):
        half = total(c).astype(BF16)
        hop1[:, c * HALF:(c + 1) * HALF] = half
        ring1_begin(2 + c, half)

    def second_total(c):
        at = slice(c * HALF, (c + 1) * HALF)
        hop2[:, at] = (2.0 * total(2 + c) - x_ref[:, at].astype(F32)).astype(BF16)

    ring1_begin(0, x_ref[:, :HALF])
    ring1_begin(1, x_ref[:, HALF:])
    for k in (2, 3, 4):
        ring1_step(0, k)
        ring1_step(1, k)
    ring1_take(0, 4)
    ring2_begin(0)
    ring1_take(1, 4)
    place_tiles()
    ring2_step(0, 2)
    ring2_step(0, 3)
    ring2_step(0, 4)
    ring2_begin(1)
    ring2_step(0, 5)
    multiply(0)
    ring2_step(1, 2)
    first_total(0)
    ring2_step(1, 3)
    ring1_step(2, 2)
    ring1_step(2, 3)
    ring2_step(1, 4)
    ring1_step(2, 4)
    ring1_take(2, 4)
    ring2_begin(2)
    ring2_step(1, 5)
    multiply(1)
    ring2_step(2, 2)
    first_total(1)
    ring2_step(2, 3)
    ring1_step(3, 2)
    ring1_step(3, 3)
    ring2_step(2, 4)
    ring1_step(3, 4)
    ring1_take(3, 4)
    ring2_begin(3)
    ring2_step(2, 5)
    multiply(2)
    ring2_step(3, 2)
    second_total(0)
    ring2_step(3, 3)
    pre_act = jnp.dot(x_ref[...], w_ref[:F], preferred_element_type=F32)
    pre_act += jnp.dot(hop1[...], w_ref[F:2 * F], preferred_element_type=F32)
    pre_act += bias_ref[...]
    ring2_step(3, 4)
    ring2_step(3, 5)
    multiply(3)
    second_total(1)

    v = pre_act + jnp.dot(hop2[...], w_ref[2 * F:], preferred_element_type=F32)
    root = 0.7978845608028654
    th = jnp.tanh(root * (v + 0.044715 * (v * v * v)))
    cdf = 0.5 * (1.0 + th)
    out_ref[...] = (v * cdf).astype(BF16)
    slope = cdf + 0.5 * v * (1.0 - th * th) * (root * (1.0 + 3.0 * 0.044715 * (v * v)))
    pre_grad = (cot_ref[...].astype(F32) * slope).astype(BF16)
    for j, part in enumerate((x_ref, hop1, hop2)):
        local = lax.dot_general(part[...], pre_grad, (((0,), (0,)), ((), ())), preferred_element_type=F32)
        for i in range(8):
            row = j * 256 + i * 32
            grad_send[row // 96, row % 96:row % 96 + 32, :] = local[i * 32:(i + 1) * 32].astype(BF16)

    def exchange(base, source, target_ref, place, count=N):
        copies = []
        for d in range(1, N):
            src, dst, target = place(d)
            copies.append(remote(src, dst, red_send.at[base, d - 1], red_recv.at[base, d - 1], target))
        for copy in copies:
            copy.wait_recv()

    exchange(0, None, None, lambda d: (
        grad_send.at[ahead(rep, d)], grad_recv.at[d - 1], (section, ahead(rep, d))))
    acc = grad_send[rep].astype(F32)
    for d in range(1, N):
        acc += grad_recv[d - 1].astype(F32)
    for i in range(24):
        y_send[i // 3, i % 3] = acc[(i // 2) * 8:(i // 2 + 1) * 8, (i % 2) * 128:(i % 2 + 1) * 128]
    exchange(1, None, None, lambda d: (
        y_send.at[ahead(y, d)], y_recv.at[d - 1], at_yz(ahead(y, d), z)))
    acc = y_send[y]
    for d in range(1, N):
        acc += y_recv[d - 1]
    z_all[z] = acc
    exchange(2, None, None, lambda d: (z_all.at[z], z_all.at[z], at_yz(y, ahead(z, d))))
    acc = z_all[0]
    for i in range(1, N):
        acc += z_all[i]
    y_all[y] = acc
    exchange(3, None, None, lambda d: (y_all.at[y], y_all.at[y], at_yz(ahead(y, d), z)))
    whole = [y_all[i // 3, i % 3] for i in range(24)]
    rep_all[rep] = jnp.concatenate(
        [jnp.concatenate([whole[2 * i], whole[2 * i + 1]], axis=1) for i in range(12)], axis=0).astype(BF16)
    exchange(4, None, None, lambda d: (rep_all.at[rep], rep_all.at[rep], (section, ahead(rep, d))))
    for i in range(N):
        grad_ref[i * 96:(i + 1) * 96, :] = rep_all[i].astype(F32)

    for copy in sends:
        copy.wait_send()


def body(node_features, tile_values, tile_rows, tile_cols, tile_counts, cheb_weights, bias, out_cotangent):
    vmem = pl.BlockSpec(memory_space=pltpu.VMEM)
    smem = pl.BlockSpec(memory_space=pltpu.SMEM)
    dma = pltpu.SemaphoreType.DMA
    scratch = (
        [pltpu.VMEM((N, N, 64, HALF), BF16)] * 8
        + [pltpu.VMEM((N, BLOCK, HALF), BF16)] * 4
        + [pltpu.VMEM((N - 1, BLOCK, HALF), BF16)] * 4
        + [
            pltpu.VMEM((N * BLOCK, TCAP * BLOCK), BF16),
            pltpu.VMEM((TCAP * BLOCK, HALF), BF16),
            pltpu.VMEM((BLOCK, F), BF16),
            pltpu.VMEM((BLOCK, F), BF16),
            pltpu.VMEM((N, 96, F), BF16),
            pltpu.VMEM((N - 1, 96, F), BF16),
            pltpu.VMEM((N, 3, 8, 128), F32),
            pltpu.VMEM((N - 1, 3, 8, 128), F32),
            pltpu.VMEM((N, 3, 8, 128), F32),
            pltpu.VMEM((N, 3, 8, 128), F32),
            pltpu.VMEM((N, 96, F), BF16),
            dma((4, 2, 2, 4)), dma((4, 2, 2, 4)),
            dma((4, 2, 2, 8)), dma((4, 2, 2, 8)),
            dma((4, N - 1)), dma((4, N - 1)),
            dma((5, N - 1)), dma((5, N - 1)),
        ]
    )
    return pl.pallas_call(
        kernel,
        out_shape=(
            jax.ShapeDtypeStruct((BLOCK, F), BF16),
            jax.ShapeDtypeStruct((3 * F, F), F32),
        ),
        in_specs=[smem] * 3 + [vmem] * 5,
        out_specs=(vmem, vmem),
        scratch_shapes=scratch,
        compiler_params=pltpu.CompilerParams(
            collective_id=0, has_side_effects=True, vmem_limit_bytes=40 * 1024 * 1024),
        cost_estimate=pl.CostEstimate(flops=2 * 10**9, bytes_accessed=4 * 10**6, transcendentals=BLOCK * F),
    )(tile_rows, tile_cols, tile_counts, node_features, tile_values, cheb_weights, bias.reshape(1, F), out_cotangent)


def solution(mesh):
    return jax.shard_map(
        body,
        mesh=mesh,
        in_specs=(
            P(("section", "rep"), None),
            P(("section", "rep"), None, None),
            P(("section", "rep")),
            P(("section", "rep")),
            P(("section", "rep")),
            P(),
            P(),
            P(("section", "rep"), None),
        ),
        out_specs=(P(("section", "rep"), None), P()),
        check_vma=False,
    )
```

time: 569 us -> 151 us (0.27)
  waiting for transfers between devices: 524 us -> 0 us
  Pallas kernels: 0 us -> 143 us
  between operations: 14.5 us -> 1.34 us
  local copies, waits for them, and re-layouts: 16.4 us -> 5.89 us
  matrix products: 10.3 us -> 0 us
    psum x1 -> x0, waiting for transfers between devices: 274 us -> none  [body(): weight_grads = lax.psum(local_grads, ('section', 'rep'))]
    all_gather x2 -> x0, waiting for transfers between devices: 176 us -> none  [propagate(): gathered = lax.all_gather(features, 'section', axis=0, tiled=True)]
    pallas_call x0 -> x1, Pallas kernels: none -> 143 us  [body(): pl.pallas_call(kernel, out_shape=(jax.ShapeDtypeStruct((BLOCK, F), BF16),...]
    reduce_scatter x2 -> x0, waiting for transfers between devices: 72.3 us -> none  [propagate(): lax.psum_scatter(summed.reshape(section_blocks * block, width), 'rep', sc...]
    dot_general x6 -> x0, matrix products: 10.3 us -> none  [the longest x2 4.79 us: propagate(): jnp.einsum('bt,tif->bif', ((tile_rows[None, :] == targets[:, None]) & liv...]
    gather x2 -> x0, local copies, waits for them, and re-layouts: 7.54 us -> none  [propagate(): picked = gathered.reshape(-1, block, width)[tile_cols]]
    dot_general x4 -> x0, local copies, waits for them, and re-layouts: 6.74 us -> none  [the longest x2 4.13 us: propagate(): jnp.einsum('tij,tjf->tif', tile_values, picked, preferred_element_type=jn...]
  transfers between devices with their start and end apart: 5 -> 0, of which waited for: 5 -> 0; matrix products, arithmetic and copies ran while one was open for 0% -> 0% of each run, Pallas kernels for 0% -> 0%
where the time goes in v1:
time: 151 us
  Pallas kernels  143 us (95%)
  local copies, waits for them, and re-layouts  5.89 us (4%)
    pallas_call x1, Pallas kernels, body(): pl.pallas_call(kernel, out_shape=(jax.ShapeDtypeStruct((BLOCK, F), BF16),...  143 us
    unnamed x16, local copies, waits for them, and re-layouts  5.89 us

profile of v1, /device:TPU:1, one launch (start us, length us, event | category | flops | bytes accessed | tf_op | source)
XLA Modules:
  0.0 150.6 jit_solution(200686937701979085)
XLA Ops:
  0.6 0.0 copy-start.6
  1.3 0.0 copy-start.4
  1.3 0.0 copy-start.5
  1.3 0.0 copy-done.6
  1.3 0.7 copy-done.4
  2.0 0.0 copy-done.5
  2.0 0.0 copy-start
  2.0 1.0 copy-done
  3.0 0.0 copy-start.1
  3.0 1.0 copy-done.1
  4.0 0.0 copy-start.2
  4.0 0.8 copy-done.2
  4.9 0.0 copy-start.3
  4.9 0.8 copy-done.3
  5.7 143.4 %shard_map.95 = (bf16[128,256]{1,0:T(8,128)(2,1)S(1)}, f32[768,256]{1,0:T(8,128)S(1)}) custom-call(s32[16]{0:T(128)S(1)} %copy-done.5, s32[16]{0:T(128)S(1)} %copy-done.6, s32[1]{0:T(128)S(6)} %copy.12.count_ref, bf16[128,256]{1,0:T(8,128)(2,1)S(1)} %copy-done.2, bf16[16,128,128]{2,1,0:T(8,128)(2,1)S(1)} %copy-done, bf16[768,256]{1,0:T(8,128)(2,1)S(1)} %copy-done.1, ...), custom_call_target="tpu_custom_call" | custom-call | flops 2000000000 | bytes 4000000 | tf_op jit(solution)/shard_map/pallas_call | solution.py:286
  149.1 0.6 copy.13
  149.7 0.9 copy.14
Async XLA Ops:
  0.6 0.7 copy-start.6
  1.3 0.7 copy-start.4
  1.3 0.7 copy-start.5
  2.0 1.0 copy-start
  3.0 1.0 copy-start.1
  4.0 0.8 copy-start.2
  4.9 0.8 copy-start.3

commit v2 on v0

v2 whole, which is shorter than its diff:
```python
import jax
import jax.numpy as jnp
from jax import lax
from jax.experimental import pallas as pl
from jax.experimental.pallas import tpu as pltpu
from jax.sharding import PartitionSpec as P

MESH = pl.DeviceIdType.MESH
N = 8
BLOCK = 128
F = 256
HALF = 128
TCAP = 16
BF16 = jnp.bfloat16
F32 = jnp.float32


RANK = (0, 1, 3, 5, 7, 6, 4, 2)
GROUPS = ((0, 1), (1, 3), (3, 5), (5, 8))
CHIPS = 4


def kernel(
    rows_ref, cols_ref, count_ref, x_hbm, tiles_hbm, w_hbm, bias_hbm, cot_hbm,
    out_ref, grad_ref,
    *scratch,
):
    gathers_a, gathers_b = scratch[0:4], scratch[4:8]
    partials, arrivals, own_sums = scratch[8:12], scratch[12:16], scratch[16:20]
    (x_ref, tiles_ref, w_ref, bias_ref, cot_ref, load_sem,
     adj, picked, hop1, hop2,
     grad_own, core_send, core_recv, x_own, x_send, x_recv, y_send, y_recv, z_all, y_all, rep_all,
     line_send, line_recv, ring_send, ring_recv, sum_send, sum_recv, red_send, red_recv) = scratch[20:]

    section = lax.axis_index("section")
    rep = lax.axis_index("rep")
    y = section // N
    z = section % N
    chip = rep // 2
    core = rep % 2
    other = 1 - core

    def ahead(pos, step):
        return lax.rem(pos + (step % N), N)

    def chip_ahead(step):
        return lax.rem(chip + step % CHIPS, CHIPS)

    def at_yz(yy, zz):
        return (yy * N + zz, rep)

    loads = [
        pltpu.make_async_copy(src, dst, load_sem.at[i])
        for i, (src, dst) in enumerate((
            (x_hbm, x_ref), (tiles_hbm, tiles_ref), (w_hbm, w_ref), (bias_hbm, bias_ref), (cot_hbm, cot_ref)))
    ]
    for load in loads:
        load.start()

    barrier = pltpu.get_barrier_semaphore()
    for d in range(1, N):
        for target in (at_yz(ahead(y, d), z), at_yz(y, ahead(z, d)), (section, ahead(rep, d))):
            pl.semaphore_signal(barrier, inc=1, device_id=target, device_id_type=MESH)

    loads[1].wait()

    def place(t, _):
        tile = tiles_ref[t]
        row = jnp.where(t < count_ref[0], rows_ref[t], N)
        for b in range(N):
            adj[b * BLOCK:(b + 1) * BLOCK, pl.ds(pl.multiple_of(t * BLOCK, BLOCK), BLOCK)] = jnp.where(
                row == b, tile, jnp.zeros_like(tile))
        return 0
    lax.fori_loop(0, TCAP, place, 0)
    for i in (0, 2, 3, 4):
        loads[i].wait()

    pl.semaphore_wait(barrier, 3 * (N - 1))

    sends = []

    def describe(src, dst, send_sem, recv_sem, target):
        return pltpu.make_async_remote_copy(
            src_ref=src, dst_ref=dst, send_sem=send_sem, recv_sem=recv_sem,
            device_id=target, device_id_type=MESH,
        )

    def remote(*args):
        copy = describe(*args)
        copy.start()
        sends.append(copy)
        return copy

    def drain():
        for copy in sends:
            copy.wait_send()
        sends.clear()

    orders = (
        (gathers_a, y, z, lambda u, v: at_yz(u, v)),
        (gathers_b, z, y, lambda u, v: at_yz(v, u)),
    )
    line, ring = {}, {}

    def ring_put(stage, g, k, o, way):
        bufs, u, v, dev = orders[o]
        first, last = GROUPS[g]
        if k == 4:
            first, last = (first, min(last, 4)) if way == 0 else (max(first, 4), last)
            if first >= last:
                return
        sign = 1 if way == 0 else -1
        group = bufs[stage].at[ahead(u, -sign * (k - 1)), pl.ds(first, last - first)]
        i = (stage, o, way, (k - 1) * 4 + g)
        ring[stage, g, k, o, way] = remote(group, group, ring_send.at[i], ring_recv.at[i], dev(ahead(u, sign), v))

    def ring_step(stage, g, k):
        for o in (0, 1):
            if k == 1:
                for j in range(*GROUPS[g]):
                    if j:
                        line[stage, o, j].wait_recv()
            for way in (0, 1):
                if (stage, g, k - 1, o, way) in ring:
                    ring[stage, g, k - 1, o, way].wait_recv()
                if k <= 4:
                    ring_put(stage, g, k, o, way)

    def gather_begin(stage, half):
        gathers_a[stage][y, 0] = half[:64]
        gathers_b[stage][z, 0] = half[64:]
        for d in (1, 7, 2, 6, 3, 5, 4):
            for o, (bufs, u, v, dev) in enumerate(orders):
                if d == 2:
                    for way in (0, 1):
                        ring_put(stage, 0, 1, o, way)
                j = RANK[-d % N]
                i = (stage, o, d - 1)
                line[stage, o, j] = remote(
                    bufs[stage].at[u, 0], bufs[stage].at[u, j], line_send.at[i], line_recv.at[i], dev(u, ahead(v, d)))

    def gather_round(stage, n):
        for g in range(4):
            k = n + 1 if g == 0 else n
            if k <= 5:
                ring_step(stage, g, k)

    def multiply(stage):
        ga, gb = gathers_a[stage], gathers_b[stage]

        def rank(d):
            d = lax.rem(d + N, N)
            return jnp.where(d <= 4, jnp.maximum(2 * d - 1, 0), 2 * (N - d))

        def pick(t, _):
            col = cols_ref[t]
            cy, cz = lax.div(col, N), lax.rem(col, N)
            at = pl.multiple_of(t * BLOCK, BLOCK)
            picked[pl.ds(at, 64), :] = ga[cy, rank(cz - z)]
            picked[pl.ds(at + 64, 64), :] = gb[cz, rank(cy - y)]
            return 0
        lax.fori_loop(0, TCAP, pick, 0, unroll=4)

        for i in (2, 1, 3, 0):
            to = chip_ahead(i)
            product = jnp.dot(
                adj[pl.ds(pl.multiple_of(to * 256, 256), 256), :], picked[...], preferred_element_type=F32)
            partials[stage][i, 0] = product[:BLOCK].astype(BF16)
            partials[stage][i, 1] = product[BLOCK:].astype(BF16)
            if i:
                for c in (0, 1):
                    remote(partials[stage].at[i, c], arrivals[stage].at[i, core],
                           sum_send.at[stage, i, c], sum_recv.at[stage, i, core], (section, to * 2 + c))
            else:
                own_sums[stage][...] = jnp.where(core == 0, product[:BLOCK], product[BLOCK:])
                remote(partials[stage].at[0, other], arrivals[stage].at[0, 0],
                       sum_send.at[stage, 0, 0], sum_recv.at[stage, 0, 0], (section, chip * 2 + other))

    def total(stage):
        acc = own_sums[stage][...]
        for i, c in ((0, 0), (1, 0), (1, 1), (3, 0), (3, 1), (2, 0), (2, 1)):
            describe(partials[stage].at[i, c], arrivals[stage].at[i, c], sum_send.at[stage, i, c],
                     sum_recv.at[stage, i, c], (section, chip * 2 + other)).wait_recv()
            acc += arrivals[stage][i, c].astype(F32)
        return acc

    def first_total(c):
        half = total(c).astype(BF16)
        hop1[:, c * HALF:(c + 1) * HALF] = half
        gather_begin(2 + c, half)

    def second_total(c):
        at = slice(c * HALF, (c + 1) * HALF)
        hop2[:, at] = (2.0 * total(2 + c) - x_ref[:, at].astype(F32)).astype(BF16)

    gather_begin(0, x_ref[:, :HALF])
    gather_round(0, 1)
    gather_begin(1, x_ref[:, HALF:])
    gather_round(0, 2)
    gather_round(1, 1)
    gather_round(0, 3)
    gather_round(0, 4)
    gather_round(1, 2)
    gather_round(0, 5)
    multiply(0)
    gather_round(1, 3)
    first_total(0)
    gather_round(1, 4)
    gather_round(2, 1)
    gather_round(1, 5)
    multiply(1)
    gather_round(2, 2)
    gather_round(2, 3)
    first_total(1)
    gather_round(2, 4)
    gather_round(3, 1)
    gather_round(2, 5)
    multiply(2)
    gather_round(3, 2)
    gather_round(3, 3)
    second_total(0)
    pre_act = jnp.dot(x_ref[...], w_ref[:F], preferred_element_type=F32)
    pre_act += jnp.dot(hop1[...], w_ref[F:2 * F], preferred_element_type=F32)
    pre_act += bias_ref[...]
    gather_round(3, 4)
    gather_round(3, 5)
    multiply(3)
    second_total(1)

    v = pre_act + jnp.dot(hop2[...], w_ref[2 * F:], preferred_element_type=F32)
    root = 0.7978845608028654
    th = jnp.tanh(root * (v + 0.044715 * (v * v * v)))
    cdf = 0.5 * (1.0 + th)
    slope = cdf + 0.5 * v * (1.0 - th * th) * (root * (1.0 + 3.0 * 0.044715 * (v * v)))
    pre_grad = (cot_ref[...].astype(F32) * slope).astype(BF16)
    for j, part in enumerate((x_ref, hop1, hop2)):
        local = lax.dot_general(part[...], pre_grad, (((0,), (0,)), ((), ())), preferred_element_type=F32)
        for i in range(8):
            row = j * 256 + i * 32
            q, at = row // 96, row % 96
            value = local[i * 32:(i + 1) * 32]
            grad_own[q // 4, q % 4, at:at + 32, :] = value
            core_send[q // 4, q % 4, at:at + 32, :] = value.astype(BF16)

    def start(step, d, src, dst, target):
        return remote(src, dst, red_send.at[step, d], red_recv.at[step, d], target)

    sibling = (section, chip * 2 + other)
    swap = start(0, 0, core_send.at[other], core_recv, sibling)
    out_ref[...] = (v * cdf).astype(BF16)
    swap.wait_recv()
    for i in range(CHIPS):
        value = grad_own[core, i] + core_recv[i].astype(F32)
        x_own[i] = value
        x_send[i] = value.astype(BF16)
    copies = [
        start(1, i, x_send.at[chip_ahead(i)], x_recv.at[i - 1], (section, chip_ahead(i) * 2 + core)) for i in (2, 1, 3)]
    acc = x_own[chip]
    for i, copy in zip((2, 1, 3), copies):
        copy.wait_recv()
        acc += x_recv[i - 1].astype(F32)
    for i in range(24):
        y_send[i // 3, i % 3] = acc[(i // 2) * 8:(i // 2 + 1) * 8, (i % 2) * 128:(i % 2 + 1) * 128]
    far = (4, 3, 5, 2, 6, 1, 7)
    copies = [start(2, d, y_send.at[ahead(y, d)], y_recv.at[d - 1], at_yz(ahead(y, d), z)) for d in far]
    drain_later = sends[:-len(far)]
    del sends[:-len(far)]
    for copy in drain_later:
        copy.wait_send()
    acc = y_send[y]
    for copy in copies:
        copy.wait_recv()
    for d in range(1, N):
        acc += y_recv[d - 1]
    z_all[z] = acc
    copies = [start(3, d, z_all.at[z], z_all.at[z], at_yz(y, ahead(z, d))) for d in far]
    for copy in copies:
        copy.wait_recv()
    acc = z_all[0]
    for i in range(1, N):
        acc += z_all[i]
    y_all[y] = jnp.concatenate([acc[0], acc[1], acc[2], jnp.zeros_like(acc[0])], axis=0).astype(BF16)
    copies = [start(4, d, y_all.at[y], y_all.at[y], at_yz(ahead(y, d), z)) for d in far]
    for copy in copies:
        copy.wait_recv()
    whole = [y_all[i // 3][(i % 3) * 8:(i % 3 + 1) * 8].astype(F32) for i in range(24)]
    rep_all[core, chip] = jnp.concatenate(
        [jnp.concatenate([whole[2 * i], whole[2 * i + 1]], axis=1) for i in range(12)], axis=0).astype(BF16)
    copies = [
        start(5, i, rep_all.at[core, chip], rep_all.at[core, chip], (section, chip_ahead(i) * 2 + core)) for i in (2, 1, 3)]
    across = [start(6, 0, rep_all.at[core, chip], rep_all.at[core, chip], sibling)]
    for i, copy in ((1, copies[1]), (3, copies[2]), (2, copies[0])):
        copy.wait_recv()
        came = rep_all.at[core, chip_ahead(-i)]
        across.append(start(6, i, came, came, sibling))
    for copy in across:
        copy.wait_recv()
    for i in range(N):
        grad_ref[i * 96:(i + 1) * 96, :] = rep_all[i // 4, i % 4]

    drain()


def body(node_features, tile_values, tile_rows, tile_cols, tile_counts, cheb_weights, bias, out_cotangent):
    vmem = pl.BlockSpec(memory_space=pltpu.VMEM)
    smem = pl.BlockSpec(memory_space=pltpu.SMEM)
    anywhere = pl.BlockSpec(memory_space=pl.ANY)
    dma = pltpu.SemaphoreType.DMA
    scratch = (
        [pltpu.VMEM((N, N, 64, HALF), BF16)] * 8
        + [pltpu.VMEM((CHIPS, 2, BLOCK, HALF), BF16)] * 8
        + [pltpu.VMEM((BLOCK, HALF), F32)] * 4
        + [
            pltpu.VMEM((BLOCK, F), BF16),
            pltpu.VMEM((TCAP, BLOCK, BLOCK), BF16),
            pltpu.VMEM((3 * F, F), BF16),
            pltpu.VMEM((1, F), F32),
            pltpu.VMEM((BLOCK, F), BF16),
            dma((5,)),
            pltpu.VMEM((N * BLOCK, TCAP * BLOCK), BF16),
            pltpu.VMEM((TCAP * BLOCK, HALF), BF16),
            pltpu.VMEM((BLOCK, F), BF16),
            pltpu.VMEM((BLOCK, F), BF16),
            pltpu.VMEM((2, CHIPS, 96, F), F32),
            pltpu.VMEM((2, CHIPS, 96, F), BF16),
            pltpu.VMEM((CHIPS, 96, F), BF16),
            pltpu.VMEM((CHIPS, 96, F), F32),
            pltpu.VMEM((CHIPS, 96, F), BF16),
            pltpu.VMEM((CHIPS - 1, 96, F), BF16),
            pltpu.VMEM((N, 3, 8, 128), F32),
            pltpu.VMEM((N - 1, 3, 8, 128), F32),
            pltpu.VMEM((N, 3, 8, 128), F32),
            pltpu.VMEM((N, 32, 128), BF16),
            pltpu.VMEM((2, CHIPS, 96, F), BF16),
            dma((4, 2, N - 1)), dma((4, 2, N - 1)),
            dma((4, 2, 2, 16)), dma((4, 2, 2, 16)),
            dma((4, CHIPS, 2)), dma((4, CHIPS, 2)),
            dma((7, N)), dma((7, N)),
        ]
    )
    layer_out, grads = pl.pallas_call(
        kernel,
        out_shape=(
            jax.ShapeDtypeStruct((BLOCK, F), BF16),
            jax.ShapeDtypeStruct((3 * F, F), BF16),
        ),
        in_specs=[smem] * 3 + [anywhere] * 5,
        out_specs=(vmem, vmem),
        scratch_shapes=scratch,
        compiler_params=pltpu.CompilerParams(
            collective_id=0, has_side_effects=True, vmem_limit_bytes=56 * 1024 * 1024),
        cost_estimate=pl.CostEstimate(flops=2 * 10**9, bytes_accessed=4 * 10**6, transcendentals=BLOCK * F),
    )(tile_rows, tile_cols, tile_counts, node_features, tile_values, cheb_weights, bias.reshape(1, F), out_cotangent)
    return layer_out, grads.astype(F32)


def solution(mesh):
    return jax.shard_map(
        body,
        mesh=mesh,
        in_specs=(
            P(("section", "rep"), None),
            P(("section", "rep"), None, None),
            P(("section", "rep")),
            P(("section", "rep")),
            P(("section", "rep")),
            P(),
            P(),
            P(("section", "rep"), None),
        ),
        out_specs=(P(("section", "rep"), None), P()),
        check_vma=False,
    )
```

time: 569 us -> 128 us (0.22)
  waiting for transfers between devices: 524 us -> 0 us
  Pallas kernels: 0 us -> 124 us
  local copies, waits for them, and re-layouts: 16.4 us -> 0.63 us
  between operations: 14.5 us -> 1.29 us
  matrix products: 10.3 us -> 0 us
    psum x1 -> x0, waiting for transfers between devices: 274 us -> none  [body(): weight_grads = lax.psum(local_grads, ('section', 'rep'))]
    all_gather x2 -> x0, waiting for transfers between devices: 176 us -> none  [propagate(): gathered = lax.all_gather(features, 'section', axis=0, tiled=True)]
    pallas_call x0 -> x1, Pallas kernels: none -> 124 us  [body(): pl.pallas_call(kernel, out_shape=(jax.ShapeDtypeStruct((BLOCK, F), BF16),...]
    reduce_scatter x2 -> x0, waiting for transfers between devices: 72.3 us -> none  [propagate(): lax.psum_scatter(summed.reshape(section_blocks * block, width), 'rep', sc...]
    dot_general x6 -> x0, matrix products: 10.3 us -> none  [the longest x2 4.79 us: propagate(): jnp.einsum('bt,tif->bif', ((tile_rows[None, :] == targets[:, None]) & liv...]
    gather x2 -> x0, local copies, waits for them, and re-layouts: 7.54 us -> none  [propagate(): picked = gathered.reshape(-1, block, width)[tile_cols]]
    dot_general x4 -> x0, local copies, waits for them, and re-layouts: 6.74 us -> none  [the longest x2 4.13 us: propagate(): jnp.einsum('tij,tjf->tif', tile_values, picked, preferred_element_type=jn...]
  transfers between devices with their start and end apart: 5 -> 0, of which waited for: 5 -> 0; matrix products, arithmetic and copies ran while one was open for 0% -> 0% of each run, Pallas kernels for 0% -> 0%
where the time goes in v2:
time: 128 us
  Pallas kernels  124 us (97%)
  other arithmetic  1.96 us (2%)
  between operations  1.29 us (1%)
    pallas_call x1, Pallas kernels, body(): pl.pallas_call(kernel, out_shape=(jax.ShapeDtypeStruct((BLOCK, F), BF16),...  124 us

profile of v2, /device:TPU:1, one launch (start us, length us, event | category | flops | bytes accessed | tf_op | source)
XLA Modules:
  0.0 128.3 jit_solution(17771553402135724421)
XLA Ops:
  1.3 124.4 %shard_map.95 = (bf16[128,256]{1,0:T(8,128)(2,1)}, bf16[768,256]{1,0:T(8,128)(2,1)}) custom-call(s32[16]{0:T(128)} %rows_ref.1, s32[16]{0:T(128)} %cols_ref.1, s32[1]{0:T(128)S(6)} %copy.11.count_ref, bf16[128,256]{1,0:T(8,128)(2,1)} %x_hbm.1, bf16[16,128,128]{2,1,0:T(8,128)(2,1)} %tiles_hbm.1, bf16[768,256]{1,0:T(8,128)(2,1)} %w_hbm.1, f32[1,256]{1,0:T(1,128)} %bitcast.1, ...), custom_call_target="tpu_custom_call" | custom-call | flops 2000000000 | bytes 4000000 | tf_op jit(solution)/shard_map/pallas_call | solution.py:341
  125.7 0.0 copy-start
  125.7 2.0 %convert_element_type.3 = f32[768,256]{1,0:T(8,128)} convert(bf16[768,256]{1,0:T(8,128)(2,1)} %get-tuple-element.5) | non-fusion elementwise | flops 196608 | bytes 1179648 | tf_op jit(solution)/shard_map/convert_element_type | solution.py:354
  127.7 0.0 copy-done
  127.7 0.6 copy.12
Async XLA Ops:
  125.7 2.0 %copy-start = (bf16[128,256]{1,0:T(8,128)(2,1)S(1)}, bf16[128,256]{1,0:T(8,128)(2,1)}, u32[]{:S(2)}) copy-start(bf16[128,256]{1,0:T(8,128)(2,1)} %get-tuple-element.8) | copy-start | bytes 196612

commit v3 on v2

--- a/solution.py
+++ b/solution.py
@@ -16,7 +16,14 @@
 
 
 RANK = (0, 1, 3, 5, 7, 6, 4, 2)
-GROUPS = ((0, 1), (1, 3), (3, 5), (5, 8))
+GROUPS = ((0, 1), (1, 3), (3, 5), (5, 7), (7, 8))
+LINE = 0
+ORDER = (
+    (0, 1, LINE), (0, 0, 1), (0, 2, LINE), (1, 1, LINE), (1, 0, 1), (1, 2, LINE), (0, 0, 2), (0, 3, LINE), (0, 1, 1), (1, 0, 2),
+    (0, 2, 1), (1, 3, LINE), (1, 1, 1), (1, 2, 1), (0, 0, 3), (0, 4, LINE), (0, 1, 2), (0, 3, 1), (1, 0, 3), (1, 4, LINE),
+    (0, 2, 2), (0, 4, 1), (1, 3, 1), (1, 1, 2), (1, 2, 2), (1, 4, 1), (0, 3, 2), (0, 1, 3), (0, 4, 2), (0, 2, 3),
+    (1, 3, 2), (1, 1, 3), (1, 4, 2), (1, 2, 3), (0, 3, 3), (0, 4, 3), (1, 3, 3), (1, 4, 3),
+)
 CHIPS = 4
 
 
@@ -77,8 +84,6 @@
 
     pl.semaphore_wait(barrier, 3 * (N - 1))
 
-    sends = []
-
     def describe(src, dst, send_sem, recv_sem, target):
         return pltpu.make_async_remote_copy(
             src_ref=src, dst_ref=dst, send_sem=send_sem, recv_sem=recv_sem,
@@ -86,64 +91,76 @@
         )
 
     def remote(*args):
-        copy = describe(*args)
-        copy.start()
-        sends.append(copy)
-        return copy
-
-    def drain():
-        for copy in sends:
-            copy.wait_send()
-        sends.clear()
+        describe(*args).start()
+
+    sibling = (section, chip * 2 + other)
+
+    def arrived(ref, sem):
+        describe(ref, ref, sem, sem, sibling).wait_recv()
+
+    def departed(ref, sem):
+        describe(ref, ref, sem, sem, sibling).wait_send()
 
     orders = (
         (gathers_a, y, z, lambda u, v: at_yz(u, v)),
         (gathers_b, z, y, lambda u, v: at_yz(v, u)),
     )
-    line, ring = {}, {}
-
-    def ring_put(stage, g, k, o, way):
+
+    def line_put(stage, o, way, dist, hops):
         bufs, u, v, dev = orders[o]
+        sign = 1 if way == 0 else -1
+        remote(bufs[stage].at[u, RANK[-sign * (dist - hops) % N]], bufs[stage].at[u, RANK[-sign * dist % N]],
+               line_send.at[stage, o], line_recv.at[stage, dist - 1], dev(u, ahead(v, sign * hops)))
+
+    def ring_put(stage, g, k):
+        for o, (bufs, u, v, dev) in enumerate(orders):
+            for way, sign in ((0, 1), (1, -1)):
+                first, last = GROUPS[g]
+                if k == 4:
+                    first, last = (first, min(last, 4)) if way == 0 else (max(first, 4), last)
+                    if first >= last:
+                        continue
+                group = bufs[stage].at[ahead(u, -sign * (k - 1)), pl.ds(first, last - first)]
+                remote(group, group, ring_send.at[stage, o], ring_recv.at[stage, g * 4 + k - 1], dev(ahead(u, sign), v))
+
+    def ring_take(stage, g, k):
         first, last = GROUPS[g]
-        if k == 4:
-            first, last = (first, min(last, 4)) if way == 0 else (max(first, 4), last)
-            if first >= last:
-                return
-        sign = 1 if way == 0 else -1
-        group = bufs[stage].at[ahead(u, -sign * (k - 1)), pl.ds(first, last - first)]
-        i = (stage, o, way, (k - 1) * 4 + g)
-        ring[stage, g, k, o, way] = remote(group, group, ring_send.at[i], ring_recv.at[i], dev(ahead(u, sign), v))
-
-    def ring_step(stage, g, k):
-        for o in (0, 1):
-            if k == 1:
-                for j in range(*GROUPS[g]):
-                    if j:
-                        line[stage, o, j].wait_recv()
-            for way in (0, 1):
-                if (stage, g, k - 1, o, way) in ring:
-                    ring[stage, g, k - 1, o, way].wait_recv()
-                if k <= 4:
-                    ring_put(stage, g, k, o, way)
+        arrived(gathers_a[stage].at[pl.ds(0, 2 if k == 4 else 4), pl.ds(first, last - first)],
+                ring_recv.at[stage, g * 4 + k - 1])
 
     def gather_begin(stage, half):
         gathers_a[stage][y, 0] = half[:64]
         gathers_b[stage][z, 0] = half[64:]
-        for d in (1, 7, 2, 6, 3, 5, 4):
-            for o, (bufs, u, v, dev) in enumerate(orders):
-                if d == 2:
+        for dist in (1, 2):
+            for o in (0, 1):
+                for way in (0, 1):
+                    line_put(stage, o, way, dist, dist)
+        ring_put(stage, 0, 1)
+
+    def gather_pair(base):
+        for c, g, k in ORDER:
+            stage = base + c
+            if k == LINE:
+                arrived(gathers_a[stage].at[pl.ds(0, 2 if g == 4 else 4), 0], line_recv.at[stage, g - 1])
+                for o in (0, 1):
                     for way in (0, 1):
-                        ring_put(stage, 0, 1, o, way)
-                j = RANK[-d % N]
-                i = (stage, o, d - 1)
-                line[stage, o, j] = remote(
-                    bufs[stage].at[u, 0], bufs[stage].at[u, j], line_send.at[i], line_recv.at[i], dev(u, ahead(v, d)))
-
-    def gather_round(stage, n):
-        for g in range(4):
-            k = n + 1 if g == 0 else n
-            if k <= 5:
-                ring_step(stage, g, k)
+                        if g == 2 or (g == 3 and way == o):
+                            line_put(stage, o, way, g + 1, 1)
+                ring_put(stage, g, 1)
+            else:
+                ring_take(stage, g, k)
+                ring_put(stage, g, k + 1)
+
+    def gather_end(stage):
+        for g in range(5):
+            ring_take(stage, g, 4)
+
+    def gather_departed(stage):
+        for o, bufs in ((0, gathers_a), (1, gathers_b)):
+            departed(bufs[stage].at[0, pl.ds(0, N - 1)], line_send.at[stage, o])
+            departed(bufs[stage].at[pl.ds(0, N - 1)], ring_send.at[stage, o])
+        departed(partials[stage].at[pl.ds(1, 3)], sum_send.at[stage, 1])
+        departed(partials[stage].at[0, 0], sum_send.at[stage, 0])
 
     def multiply(stage):
         ga, gb = gathers_a[stage], gathers_b[stage]
@@ -170,18 +187,19 @@
             if i:
                 for c in (0, 1):
                     remote(partials[stage].at[i, c], arrivals[stage].at[i, core],
-                           sum_send.at[stage, i, c], sum_recv.at[stage, i, core], (section, to * 2 + c))
+                           sum_send.at[stage, 1], sum_recv.at[stage, 1], (section, to * 2 + c))
             else:
                 own_sums[stage][...] = jnp.where(core == 0, product[:BLOCK], product[BLOCK:])
                 remote(partials[stage].at[0, other], arrivals[stage].at[0, 0],
-                       sum_send.at[stage, 0, 0], sum_recv.at[stage, 0, 0], (section, chip * 2 + other))
+                       sum_send.at[stage, 0], sum_recv.at[stage, 0], sibling)
 
     def total(stage):
-        acc = own_sums[stage][...]
-        for i, c in ((0, 0), (1, 0), (1, 1), (3, 0), (3, 1), (2, 0), (2, 1)):
-            describe(partials[stage].at[i, c], arrivals[stage].at[i, c], sum_send.at[stage, i, c],
-                     sum_recv.at[stage, i, c], (section, chip * 2 + other)).wait_recv()
-            acc += arrivals[stage][i, c].astype(F32)
+        arrived(arrivals[stage].at[0, 0], sum_recv.at[stage, 0])
+        acc = own_sums[stage][...] + arrivals[stage][0, 0].astype(F32)
+        arrived(arrivals[stage].at[pl.ds(1, 3)], sum_recv.at[stage, 1])
+        for i in (1, 2, 3):
+            for c in (0, 1):
+                acc += arrivals[stage][i, c].astype(F32)
         return acc
 
     def first_total(c):
@@ -194,37 +212,23 @@
         hop2[:, at] = (2.0 * total(2 + c) - x_ref[:, at].astype(F32)).astype(BF16)
 
     gather_begin(0, x_ref[:, :HALF])
-    gather_round(0, 1)
     gather_begin(1, x_ref[:, HALF:])
-    gather_round(0, 2)
-    gather_round(1, 1)
-    gather_round(0, 3)
-    gather_round(0, 4)
-    gather_round(1, 2)
-    gather_round(0, 5)
+    gather_pair(0)
+    gather_end(0)
     multiply(0)
-    gather_round(1, 3)
+    gather_end(1)
+    multiply(1)
     first_total(0)
-    gather_round(1, 4)
-    gather_round(2, 1)
-    gather_round(1, 5)
-    multiply(1)
-    gather_round(2, 2)
-    gather_round(2, 3)
     first_total(1)
-    gather_round(2, 4)
-    gather_round(3, 1)
-    gather_round(2, 5)
+    gather_pair(2)
+    gather_end(2)
     multiply(2)
-    gather_round(3, 2)
-    gather_round(3, 3)
-    second_total(0)
+    gather_end(3)
+    multiply(3)
     pre_act = jnp.dot(x_ref[...], w_ref[:F], preferred_element_type=F32)
     pre_act += jnp.dot(hop1[...], w_ref[F:2 * F], preferred_element_type=F32)
     pre_act += bias_ref[...]
-    gather_round(3, 4)
-    gather_round(3, 5)
-    multiply(3)
+    second_total(0)
     second_total(1)
 
     v = pre_act + jnp.dot(hop2[...], w_ref[2 * F:], preferred_element_type=F32)
@@ -242,63 +246,67 @@
             grad_own[q // 4, q % 4, at:at + 32, :] = value
             core_send[q // 4, q % 4, at:at + 32, :] = value.astype(BF16)
 
-    def start(step, d, src, dst, target):
-        return remote(src, dst, red_send.at[step, d], red_recv.at[step, d], target)
-
-    sibling = (section, chip * 2 + other)
-    swap = start(0, 0, core_send.at[other], core_recv, sibling)
+    def start(send, recv, src, dst, target):
+        remote(src, dst, red_send.at[send], red_recv.at[recv], target)
+
+    start(0, 0, core_send.at[other], core_recv, sibling)
     out_ref[...] = (v * cdf).astype(BF16)
-    swap.wait_recv()
+    arrived(core_recv, red_recv.at[0])
     for i in range(CHIPS):
         value = grad_own[core, i] + core_recv[i].astype(F32)
         x_own[i] = value
         x_send[i] = value.astype(BF16)
-    copies = [
-        start(1, i, x_send.at[chip_ahead(i)], x_recv.at[i - 1], (section, chip_ahead(i) * 2 + core)) for i in (2, 1, 3)]
+    for i in (2, 1, 3):
+        start(1, 1, x_send.at[chip_ahead(i)], x_recv.at[i - 1], (section, chip_ahead(i) * 2 + core))
+    departed(core_send.at[0], red_send.at[0])
+    gather_departed(0)
+    gather_departed(1)
+    arrived(x_recv, red_recv.at[1])
     acc = x_own[chip]
-    for i, copy in zip((2, 1, 3), copies):
-        copy.wait_recv()
-        acc += x_recv[i - 1].astype(F32)
+    for i in range(CHIPS - 1):
+        acc += x_recv[i].astype(F32)
     for i in range(24):
         y_send[i // 3, i % 3] = acc[(i // 2) * 8:(i // 2 + 1) * 8, (i % 2) * 128:(i % 2 + 1) * 128]
     far = (4, 3, 5, 2, 6, 1, 7)
-    copies = [start(2, d, y_send.at[ahead(y, d)], y_recv.at[d - 1], at_yz(ahead(y, d), z)) for d in far]
-    drain_later = sends[:-len(far)]
-    del sends[:-len(far)]
-    for copy in drain_later:
-        copy.wait_send()
+    for d in far:
+        start(2, 2, y_send.at[ahead(y, d)], y_recv.at[d - 1], at_yz(ahead(y, d), z))
+    departed(x_send.at[pl.ds(0, CHIPS - 1)], red_send.at[1])
+    gather_departed(2)
+    gather_departed(3)
     acc = y_send[y]
-    for copy in copies:
-        copy.wait_recv()
+    arrived(y_recv, red_recv.at[2])
     for d in range(1, N):
         acc += y_recv[d - 1]
     z_all[z] = acc
-    copies = [start(3, d, z_all.at[z], z_all.at[z], at_yz(y, ahead(z, d))) for d in far]
-    for copy in copies:
-        copy.wait_recv()
+    for d in far:
+        start(3, 3, z_all.at[z], z_all.at[z], at_yz(y, ahead(z, d)))
+    arrived(z_all.at[pl.ds(0, N - 1)], red_recv.at[3])
     acc = z_all[0]
     for i in range(1, N):
         acc += z_all[i]
     y_all[y] = jnp.concatenate([acc[0], acc[1], acc[2], jnp.zeros_like(acc[0])], axis=0).astype(BF16)
-    copies = [start(4, d, y_all.at[y], y_all.at[y], at_yz(ahead(y, d), z)) for d in far]
-    for copy in copies:
-        copy.wait_recv()
+    for d in far:
+        start(4, 4, y_all.at[y], y_all.at[y], at_yz(ahead(y, d), z))
+    departed(y_recv, red_send.at[2])
+    departed(z_all.at[pl.ds(0, N - 1)], red_send.at[3])
+    arrived(y_all.at[pl.ds(0, N - 1)], red_recv.at[4])
     whole = [y_all[i // 3][(i % 3) * 8:(i % 3 + 1) * 8].astype(F32) for i in range(24)]
     rep_all[core, chip] = jnp.concatenate(
         [jnp.concatenate([whole[2 * i], whole[2 * i + 1]], axis=1) for i in range(12)], axis=0).astype(BF16)
-    copies = [
-        start(5, i, rep_all.at[core, chip], rep_all.at[core, chip], (section, chip_ahead(i) * 2 + core)) for i in (2, 1, 3)]
-    across = [start(6, 0, rep_all.at[core, chip], rep_all.at[core, chip], sibling)]
-    for i, copy in ((1, copies[1]), (3, copies[2]), (2, copies[0])):
-        copy.wait_recv()
+    mine = rep_all.at[core, chip]
+    for i in (2, 1, 3):
+        start(5, 5 + i, mine, mine, (section, chip_ahead(i) * 2 + core))
+    start(6, 5, mine, mine, sibling)
+    departed(y_all.at[pl.ds(0, N - 1)], red_send.at[4])
+    for i in (1, 3, 2):
         came = rep_all.at[core, chip_ahead(-i)]
-        across.append(start(6, i, came, came, sibling))
-    for copy in across:
-        copy.wait_recv()
+        arrived(came, red_recv.at[5 + i])
+        start(6, 5, came, came, sibling)
+    arrived(rep_all.at[other], red_recv.at[5])
     for i in range(N):
-        grad_ref[i * 96:(i + 1) * 96, :] = rep_all[i // 4, i % 4]
-
-    drain()
+        grad_ref[i * 96:(i + 1) * 96, :] = rep_all[i // 4, i % 4].astype(F32)
+    departed(rep_all.at[0, pl.ds(0, CHIPS - 1)], red_send.at[5])
+    departed(rep_all.at[0], red_send.at[6])
 
 
 def body(node_features, tile_values, tile_rows, tile_cols, tile_counts, cheb_weights, bias, out_cotangent):
@@ -332,17 +340,17 @@
             pltpu.VMEM((N, 3, 8, 128), F32),
             pltpu.VMEM((N, 32, 128), BF16),
             pltpu.VMEM((2, CHIPS, 96, F), BF16),
-            dma((4, 2, N - 1)), dma((4, 2, N - 1)),
-            dma((4, 2, 2, 16)), dma((4, 2, 2, 16)),
-            dma((4, CHIPS, 2)), dma((4, CHIPS, 2)),
-            dma((7, N)), dma((7, N)),
+            dma((4, 2)), dma((4, 4)),
+            dma((4, 2)), dma((4, 20)),
+            dma((4, 2)), dma((4, 2)),
+            dma((7,)), dma((9,)),
         ]
     )
-    layer_out, grads = pl.pallas_call(
+    return pl.pallas_call(
         kernel,
         out_shape=(
             jax.ShapeDtypeStruct((BLOCK, F), BF16),
-            jax.ShapeDtypeStruct((3 * F, F), BF16),
+            jax.ShapeDtypeStruct((3 * F, F), F32),
         ),
         in_specs=[smem] * 3 + [anywhere] * 5,
         out_specs=(vmem, vmem),
@@ -351,7 +359,6 @@
             collective_id=0, has_side_effects=True, vmem_limit_bytes=56 * 1024 * 1024),
         cost_estimate=pl.CostEstimate(flops=2 * 10**9, bytes_accessed=4 * 10**6, transcendentals=BLOCK * F),
     )(tile_rows, tile_cols, tile_counts, node_features, tile_values, cheb_weights, bias.reshape(1, F), out_cotangent)
-    return layer_out, grads.astype(F32)
 
 
 def solution(mesh):

time: 128 us -> 118 us (0.922)
  Pallas kernels: 124 us -> 113 us
  local copies, waits for them, and re-layouts: 0.63 us -> 3.54 us
  other arithmetic: 1.96 us -> 0 us
    pallas_call x1, Pallas kernels: 124 us -> 113 us  [body(): pl.pallas_call(kernel, out_shape=(jax.ShapeDtypeStruct((BLOCK, F), BF16),...]
    unnamed x3 -> x2, local copies, waits for them, and re-layouts: 0.63 us -> 3.54 us
    convert_element_type x1 -> x0, other arithmetic: 1.96 us -> none  [body(): return (layer_out, grads.astype(F32))]
where the time goes in v3:
time: 118 us; the launch traced here: 117 us
  Pallas kernels  113 us (96%)
  local copies, waits for them, and re-layouts  3.54 us (3%)
  between operations  1.29 us (1%)
    pallas_call x1, Pallas kernels, body(): pl.pallas_call(kernel, out_shape=(jax.ShapeDtypeStruct((BLOCK, F), BF16),...  113 us
    unnamed x2, local copies, waits for them, and re-layouts  3.54 us

profile of v3, /device:TPU:1, one launch (start us, length us, event | category | flops | bytes accessed | tf_op | source)
XLA Modules:
  0.0 117.5 jit_solution(13194245898208099245)
XLA Ops:
  1.3 112.7 %shard_map.95 = (bf16[128,256]{1,0:T(8,128)(2,1)}, f32[768,256]{1,0:T(8,128)}) custom-call(s32[16]{0:T(128)} %rows_ref.1, s32[16]{0:T(128)} %cols_ref.1, s32[1]{0:T(128)S(6)} %copy.12.count_ref, bf16[128,256]{1,0:T(8,128)(2,1)} %x_hbm.1, bf16[16,128,128]{2,1,0:T(8,128)(2,1)} %tiles_hbm.1, bf16[768,256]{1,0:T(8,128)(2,1)} %w_hbm.1, f32[1,256]{1,0:T(1,128)} %bitcast.1, ...), custom_call_target="tpu_custom_call" | custom-call | flops 2000000000 | bytes 4000000 | tf_op jit(solution)/shard_map/pallas_call | solution.py:349
  114.0 1.5 %copy.13 = bf16[128,256]{1,0:T(8,128)(2,1)} copy(bf16[128,256]{1,0:T(8,128)(2,1)} %get-tuple-element.4) | data formatting | bytes 131072
  115.4 2.1 %copy.14 = f32[768,256]{1,0:T(8,128)} copy(f32[768,256]{1,0:T(8,128)} %get-tuple-element.5) | data formatting | bytes 1572864

commit v4 on v3

--- a/solution.py
+++ b/solution.py
@@ -36,7 +36,7 @@
     partials, arrivals, own_sums = scratch[8:12], scratch[12:16], scratch[16:20]
     (x_ref, tiles_ref, w_ref, bias_ref, cot_ref, load_sem,
      adj, picked, hop1, hop2,
-     grad_own, core_send, core_recv, x_own, x_send, x_recv, y_send, y_recv, z_all, y_all, rep_all,
+     grad_own, core_send, core_recv, x_send, x_recv, y_send, y_recv, z_all, y_all, rep_all,
      line_send, line_recv, ring_send, ring_recv, sum_send, sum_recv, red_send, red_recv) = scratch[20:]
 
     section = lax.axis_index("section")
@@ -237,76 +237,85 @@
     cdf = 0.5 * (1.0 + th)
     slope = cdf + 0.5 * v * (1.0 - th * th) * (root * (1.0 + 3.0 * 0.044715 * (v * v)))
     pre_grad = (cot_ref[...].astype(F32) * slope).astype(BF16)
-    for j, part in enumerate((x_ref, hop1, hop2)):
-        local = lax.dot_general(part[...], pre_grad, (((0,), (0,)), ((), ())), preferred_element_type=F32)
+
+    def start(part, send, recv, src, dst, target):
+        remote(src, dst, red_send.at[part, send], red_recv.at[part, recv], target)
+
+    parts = range(3)
+    others = (2, 1, 3)
+    far = (4, 3, 5, 2, 6, 1, 7)
+    for p, block in enumerate((x_ref, hop1, hop2)):
+        local = lax.dot_general(block[...], pre_grad, (((0,), (0,)), ((), ())), preferred_element_type=F32)
         for i in range(8):
-            row = j * 256 + i * 32
-            q, at = row // 96, row % 96
             value = local[i * 32:(i + 1) * 32]
-            grad_own[q // 4, q % 4, at:at + 32, :] = value
-            core_send[q // 4, q % 4, at:at + 32, :] = value.astype(BF16)
-
-    def start(send, recv, src, dst, target):
-        remote(src, dst, red_send.at[send], red_recv.at[recv], target)
-
-    start(0, 0, core_send.at[other], core_recv, sibling)
+            grad_own[p, i // CHIPS, i % CHIPS] = value
+            core_send[p, i // CHIPS, i % CHIPS] = value.astype(BF16)
+        start(p, 0, 0, core_send.at[p, other], core_recv.at[p], sibling)
     out_ref[...] = (v * cdf).astype(BF16)
-    arrived(core_recv, red_recv.at[0])
-    for i in range(CHIPS):
-        value = grad_own[core, i] + core_recv[i].astype(F32)
-        x_own[i] = value
-        x_send[i] = value.astype(BF16)
-    for i in (2, 1, 3):
-        start(1, 1, x_send.at[chip_ahead(i)], x_recv.at[i - 1], (section, chip_ahead(i) * 2 + core))
-    departed(core_send.at[0], red_send.at[0])
+    for p in parts:
+        arrived(core_recv.at[p], red_recv.at[p, 0])
+        for i in others:
+            to = chip_ahead(i)
+            x_send[p, i - 1] = (grad_own[p, core, to] + core_recv[p, to].astype(F32)).astype(BF16)
+            start(p, 1, 1, x_send.at[p, i - 1], x_recv.at[p, i - 1], (section, to * 2 + core))
     gather_departed(0)
     gather_departed(1)
-    arrived(x_recv, red_recv.at[1])
-    acc = x_own[chip]
-    for i in range(CHIPS - 1):
-        acc += x_recv[i].astype(F32)
-    for i in range(24):
-        y_send[i // 3, i % 3] = acc[(i // 2) * 8:(i // 2 + 1) * 8, (i % 2) * 128:(i % 2 + 1) * 128]
-    far = (4, 3, 5, 2, 6, 1, 7)
-    for d in far:
-        start(2, 2, y_send.at[ahead(y, d)], y_recv.at[d - 1], at_yz(ahead(y, d), z))
-    departed(x_send.at[pl.ds(0, CHIPS - 1)], red_send.at[1])
+    for p in parts:
+        acc = grad_own[p, core, chip] + core_recv[p, chip].astype(F32)
+        arrived(x_recv.at[p], red_recv.at[p, 1])
+        for i in range(CHIPS - 1):
+            acc += x_recv[p, i].astype(F32)
+        for i in range(N):
+            y_send[p, i] = acc[(i // 2) * 8:(i // 2 + 1) * 8, (i % 2) * 128:(i % 2 + 1) * 128]
+        for d in far:
+            start(p, 2, 2, y_send.at[p, ahead(y, d)], y_recv.at[p, d - 1], at_yz(ahead(y, d), z))
     gather_departed(2)
     gather_departed(3)
-    acc = y_send[y]
-    arrived(y_recv, red_recv.at[2])
-    for d in range(1, N):
-        acc += y_recv[d - 1]
-    z_all[z] = acc
-    for d in far:
-        start(3, 3, z_all.at[z], z_all.at[z], at_yz(y, ahead(z, d)))
-    arrived(z_all.at[pl.ds(0, N - 1)], red_recv.at[3])
-    acc = z_all[0]
-    for i in range(1, N):
-        acc += z_all[i]
-    y_all[y] = jnp.concatenate([acc[0], acc[1], acc[2], jnp.zeros_like(acc[0])], axis=0).astype(BF16)
-    for d in far:
-        start(4, 4, y_all.at[y], y_all.at[y], at_yz(ahead(y, d), z))
-    departed(y_recv, red_send.at[2])
-    departed(z_all.at[pl.ds(0, N - 1)], red_send.at[3])
-    arrived(y_all.at[pl.ds(0, N - 1)], red_recv.at[4])
-    whole = [y_all[i // 3][(i % 3) * 8:(i % 3 + 1) * 8].astype(F32) for i in range(24)]
-    rep_all[core, chip] = jnp.concatenate(
-        [jnp.concatenate([whole[2 * i], whole[2 * i + 1]], axis=1) for i in range(12)], axis=0).astype(BF16)
-    mine = rep_all.at[core, chip]
-    for i in (2, 1, 3):
-        start(5, 5 + i, mine, mine, (section, chip_ahead(i) * 2 + core))
-    start(6, 5, mine, mine, sibling)
-    departed(y_all.at[pl.ds(0, N - 1)], red_send.at[4])
-    for i in (1, 3, 2):
-        came = rep_all.at[core, chip_ahead(-i)]
-        arrived(came, red_recv.at[5 + i])
-        start(6, 5, came, came, sibling)
-    arrived(rep_all.at[other], red_recv.at[5])
-    for i in range(N):
-        grad_ref[i * 96:(i + 1) * 96, :] = rep_all[i // 4, i % 4].astype(F32)
-    departed(rep_all.at[0, pl.ds(0, CHIPS - 1)], red_send.at[5])
-    departed(rep_all.at[0], red_send.at[6])
+    for p in parts:
+        acc = y_send[p, y]
+        arrived(y_recv.at[p], red_recv.at[p, 2])
+        for d in range(1, N):
+            acc += y_recv[p, d - 1]
+        z_all[p, z] = acc
+        for d in far:
+            start(p, 3, 3, z_all.at[p, z], z_all.at[p, z], at_yz(y, ahead(z, d)))
+    for p in parts:
+        departed(core_send.at[p, 0], red_send.at[p, 0])
+        departed(x_send.at[p], red_send.at[p, 1])
+        departed(y_recv.at[p], red_send.at[p, 2])
+    for p in parts:
+        arrived(z_all.at[p, pl.ds(0, N - 1)], red_recv.at[p, 3])
+        acc = z_all[p, 0]
+        for i in range(1, N):
+            acc += z_all[p, i]
+        y_all[p, y] = acc
+        for d in far:
+            start(p, 4, 4, y_all.at[p, y], y_all.at[p, y], at_yz(ahead(y, d), z))
+    for p in parts:
+        departed(z_all.at[p, pl.ds(0, N - 1)], red_send.at[p, 3])
+    for p in parts:
+        arrived(y_all.at[p, pl.ds(0, N - 1)], red_recv.at[p, 4])
+        rep_all[p, core, chip] = jnp.concatenate(
+            [jnp.concatenate([y_all[p, 2 * i], y_all[p, 2 * i + 1]], axis=1) for i in range(4)], axis=0).astype(BF16)
+        mine = rep_all.at[p, core, chip]
+        for i in others:
+            start(p, 5, 5 + i, mine, mine, (section, chip_ahead(i) * 2 + core))
+        start(p, 6, 5, mine, mine, sibling)
+    for p in parts:
+        departed(y_all.at[p, pl.ds(0, N - 1)], red_send.at[p, 4])
+    for p in parts:
+        for i in (1, 3, 2):
+            came = rep_all.at[p, core, chip_ahead(-i)]
+            arrived(came, red_recv.at[p, 5 + i])
+            start(p, 6, 5, came, came, sibling)
+    for p in parts:
+        arrived(rep_all.at[p, other], red_recv.at[p, 5])
+        for i in range(N):
+            at = p * F + i * 32
+            grad_ref[at:at + 32, :] = rep_all[p, i // CHIPS, i % CHIPS].astype(F32)
+    for p in parts:
+        departed(rep_all.at[p, 0, pl.ds(0, CHIPS - 1)], red_send.at[p, 5])
+        departed(rep_all.at[p, 0], red_send.at[p, 6])
 
 
 def body(node_features, tile_values, tile_rows, tile_cols, tile_counts, cheb_weights, bias, out_cotangent):
@@ -329,21 +338,20 @@
             pltpu.VMEM((TCAP * BLOCK, HALF), BF16),
             pltpu.VMEM((BLOCK, F), BF16),
             pltpu.VMEM((BLOCK, F), BF16),
-            pltpu.VMEM((2, CHIPS, 96, F), F32),
-            pltpu.VMEM((2, CHIPS, 96, F), BF16),
-            pltpu.VMEM((CHIPS, 96, F), BF16),
-            pltpu.VMEM((CHIPS, 96, F), F32),
-            pltpu.VMEM((CHIPS, 96, F), BF16),
-            pltpu.VMEM((CHIPS - 1, 96, F), BF16),
-            pltpu.VMEM((N, 3, 8, 128), F32),
-            pltpu.VMEM((N - 1, 3, 8, 128), F32),
-            pltpu.VMEM((N, 3, 8, 128), F32),
-            pltpu.VMEM((N, 32, 128), BF16),
-            pltpu.VMEM((2, CHIPS, 96, F), BF16),
+            pltpu.VMEM((3, 2, CHIPS, 32, F), F32),
+            pltpu.VMEM((3, 2, CHIPS, 32, F), BF16),
+            pltpu.VMEM((3, CHIPS, 32, F), BF16),
+            pltpu.VMEM((3, CHIPS - 1, 32, F), BF16),
+            pltpu.VMEM((3, CHIPS - 1, 32, F), BF16),
+            pltpu.VMEM((3, N, 8, 128), F32),
+            pltpu.VMEM((3, N - 1, 8, 128), F32),
+            pltpu.VMEM((3, N, 8, 128), F32),
+            pltpu.VMEM((3, N, 8, 128), F32),
+            pltpu.VMEM((3, 2, CHIPS, 32, F), BF16),
             dma((4, 2)), dma((4, 4)),
             dma((4, 2)), dma((4, 20)),
             dma((4, 2)), dma((4, 2)),
-            dma((7,)), dma((9,)),
+            dma((3, 7)), dma((3, 9)),
         ]
     )
     return pl.pallas_call(

time: 118 us -> 116 us (0.983)
  Pallas kernels: 113 us -> 111 us
    pallas_call x1, Pallas kernels: 113 us -> 111 us  [body(): pl.pallas_call(kernel, out_shape=(jax.ShapeDtypeStruct((BLOCK, F), BF16),...]
where the time goes in v4:
time: 116 us
  Pallas kernels  111 us (96%)
  local copies, waits for them, and re-layouts  3.54 us (3%)
  between operations  1.29 us (1%)
    pallas_call x1, Pallas kernels, body(): pl.pallas_call(kernel, out_shape=(jax.ShapeDtypeStruct((BLOCK, F), BF16),...  111 us
    unnamed x2, local copies, waits for them, and re-layouts  3.54 us

profile of v4, /device:TPU:1, one launch (start us, length us, event | category | flops | bytes accessed | tf_op | source)
XLA Modules:
  0.0 115.9 jit_solution(13790386922161827803)
XLA Ops:
  1.3 111.1 %shard_map.95 = (bf16[128,256]{1,0:T(8,128)(2,1)}, f32[768,256]{1,0:T(8,128)}) custom-call(s32[16]{0:T(128)} %rows_ref.1, s32[16]{0:T(128)} %cols_ref.1, s32[1]{0:T(128)S(6)} %copy.12.count_ref, bf16[128,256]{1,0:T(8,128)(2,1)} %x_hbm.1, bf16[16,128,128]{2,1,0:T(8,128)(2,1)} %tiles_hbm.1, bf16[768,256]{1,0:T(8,128)(2,1)} %w_hbm.1, f32[1,256]{1,0:T(1,128)} %bitcast.1, ...), custom_call_target="tpu_custom_call" | custom-call | flops 2000000000 | bytes 4000000 | tf_op jit(solution)/shard_map/pallas_call | solution.py:357
  112.4 1.5 %copy.13 = bf16[128,256]{1,0:T(8,128)(2,1)} copy(bf16[128,256]{1,0:T(8,128)(2,1)} %get-tuple-element.4) | data formatting | bytes 131072
  113.9 2.1 %copy.14 = f32[768,256]{1,0:T(8,128)} copy(f32[768,256]{1,0:T(8,128)} %get-tuple-element.5) | data formatting | bytes 1572864

commit v5 on v4

--- a/solution.py
+++ b/solution.py
@@ -65,9 +65,11 @@
         load.start()
 
     barrier = pltpu.get_barrier_semaphore()
-    for d in range(1, N):
-        for target in (at_yz(ahead(y, d), z), at_yz(y, ahead(z, d)), (section, ahead(rep, d))):
-            pl.semaphore_signal(barrier, inc=1, device_id=target, device_id_type=MESH)
+    near = [(section, ahead(rep, d)) for d in range(1, N)]
+    for d in (1, 2, -1, -2):
+        near += [at_yz(ahead(y, d), z), at_yz(y, ahead(z, d))]
+    for target in near:
+        pl.semaphore_signal(barrier, inc=1, device_id=target, device_id_type=MESH)
 
     loads[1].wait()
 
@@ -82,7 +84,7 @@
     for i in (0, 2, 3, 4):
         loads[i].wait()
 
-    pl.semaphore_wait(barrier, 3 * (N - 1))
+    pl.semaphore_wait(barrier, len(near))
 
     def describe(src, dst, send_sem, recv_sem, target):
         return pltpu.make_async_remote_copy(

time: 116 us -> 115 us (level)
    pallas_call x1, Pallas kernels: 111 us -> 110 us  [body(): pl.pallas_call(kernel, out_shape=(jax.ShapeDtypeStruct((BLOCK, F), BF16),...]
where the time goes in v5:
time: 115 us; the launch traced here: 114 us
  Pallas kernels  110 us (96%)
  local copies, waits for them, and re-layouts  3.54 us (3%)
  between operations  1.29 us (1%)
    pallas_call x1, Pallas kernels, body(): pl.pallas_call(kernel, out_shape=(jax.ShapeDtypeStruct((BLOCK, F), BF16),...  110 us
    unnamed x2, local copies, waits for them, and re-layouts  3.54 us

profile of v5, /device:TPU:1, one launch (start us, length us, event | category | flops | bytes accessed | tf_op | source)
XLA Modules:
  0.0 114.4 jit_solution(11256355804207986167)
XLA Ops:
  1.3 109.6 %shard_map.95 = (bf16[128,256]{1,0:T(8,128)(2,1)}, f32[768,256]{1,0:T(8,128)}) custom-call(s32[16]{0:T(128)} %rows_ref.1, s32[16]{0:T(128)} %cols_ref.1, s32[1]{0:T(128)S(6)} %copy.12.count_ref, bf16[128,256]{1,0:T(8,128)(2,1)} %x_hbm.1, bf16[16,128,128]{2,1,0:T(8,128)(2,1)} %tiles_hbm.1, bf16[768,256]{1,0:T(8,128)(2,1)} %w_hbm.1, f32[1,256]{1,0:T(1,128)} %bitcast.1, ...), custom_call_target="tpu_custom_call" | custom-call | flops 2000000000 | bytes 4000000 | tf_op jit(solution)/shard_map/pallas_call | solution.py:359
  110.9 1.5 %copy.13 = bf16[128,256]{1,0:T(8,128)(2,1)} copy(bf16[128,256]{1,0:T(8,128)(2,1)} %get-tuple-element.4) | data formatting | bytes 131072
  112.3 2.1 %copy.14 = f32[768,256]{1,0:T(8,128)} copy(f32[768,256]{1,0:T(8,128)} %get-tuple-element.5) | data formatting | bytes 1572864

commit v6 on v5

--- a/solution.py
+++ b/solution.py
@@ -29,13 +29,13 @@
 
 def kernel(
     rows_ref, cols_ref, count_ref, x_hbm, tiles_hbm, w_hbm, bias_hbm, cot_hbm,
-    out_ref, grad_ref,
+    out_hbm, grad_hbm,
     *scratch,
 ):
     gathers_a, gathers_b = scratch[0:4], scratch[4:8]
     partials, arrivals, own_sums = scratch[8:12], scratch[12:16], scratch[16:20]
     (x_ref, tiles_ref, w_ref, bias_ref, cot_ref, load_sem,
-     adj, picked, hop1, hop2,
+     adj, picked, hop1, hop2, out_ref, grad_ref, store_sem,
      grad_own, core_send, core_recv, x_send, x_recv, y_send, y_recv, z_all, y_all, rep_all,
      line_send, line_recv, ring_send, ring_recv, sum_send, sum_recv, red_send, red_recv) = scratch[20:]
 
@@ -254,6 +254,8 @@
             core_send[p, i // CHIPS, i % CHIPS] = value.astype(BF16)
         start(p, 0, 0, core_send.at[p, other], core_recv.at[p], sibling)
     out_ref[...] = (v * cdf).astype(BF16)
+    stores = [pltpu.make_async_copy(out_ref, out_hbm, store_sem.at[3])]
+    stores[0].start()
     for p in parts:
         arrived(core_recv.at[p], red_recv.at[p, 0])
         for i in others:
@@ -315,13 +317,17 @@
         for i in range(N):
             at = p * F + i * 32
             grad_ref[at:at + 32, :] = rep_all[p, i // CHIPS, i % CHIPS].astype(F32)
+        rows = pl.ds(p * F, F)
+        stores.append(pltpu.make_async_copy(grad_ref.at[rows], grad_hbm.at[rows], store_sem.at[p]))
+        stores[-1].start()
     for p in parts:
         departed(rep_all.at[p, 0, pl.ds(0, CHIPS - 1)], red_send.at[p, 5])
         departed(rep_all.at[p, 0], red_send.at[p, 6])
+    for store in stores:
+        store.wait()
 
 
 def body(node_features, tile_values, tile_rows, tile_cols, tile_counts, cheb_weights, bias, out_cotangent):
-    vmem = pl.BlockSpec(memory_space=pltpu.VMEM)
     smem = pl.BlockSpec(memory_space=pltpu.SMEM)
     anywhere = pl.BlockSpec(memory_space=pl.ANY)
     dma = pltpu.SemaphoreType.DMA
@@ -340,6 +346,9 @@
             pltpu.VMEM((TCAP * BLOCK, HALF), BF16),
             pltpu.VMEM((BLOCK, F), BF16),
             pltpu.VMEM((BLOCK, F), BF16),
+            pltpu.VMEM((BLOCK, F), BF16),
+            pltpu.VMEM((3 * F, F), F32),
+            dma((4,)),
             pltpu.VMEM((3, 2, CHIPS, 32, F), F32),
             pltpu.VMEM((3, 2, CHIPS, 32, F), BF16),
             pltpu.VMEM((3, CHIPS, 32, F), BF16),
@@ -363,7 +372,7 @@
             jax.ShapeDtypeStruct((3 * F, F), F32),
         ),
         in_specs=[smem] * 3 + [anywhere] * 5,
-        out_specs=(vmem, vmem),
+        out_specs=(anywhere, anywhere),
         scratch_shapes=scratch,
         compiler_params=pltpu.CompilerParams(
             collective_id=0, has_side_effects=True, vmem_limit_bytes=56 * 1024 * 1024),

time: 115 us -> 115 us (level)
  no operation moved by 1% of the time
where the time goes in v6:
time: 115 us; the launch traced here: 114 us
  Pallas kernels  109 us (95%)
  local copies, waits for them, and re-layouts  3.54 us (3%)
  between operations  1.29 us (1%)
    pallas_call x1, Pallas kernels, body(): pl.pallas_call(kernel, out_shape=(jax.ShapeDtypeStruct((BLOCK, F), BF16),...  109 us
    unnamed x2, local copies, waits for them, and re-layouts  3.54 us

profile of v6, /device:TPU:1, one launch (start us, length us, event | category | flops | bytes accessed | tf_op | source)
XLA Modules:
  0.0 114.3 jit_solution(16050241104551032270)
XLA Ops:
  1.3 109.5 %shard_map.95 = (bf16[128,256]{1,0:T(8,128)(2,1)}, f32[768,256]{1,0:T(8,128)}) custom-call(s32[16]{0:T(128)} %rows_ref.1, s32[16]{0:T(128)} %cols_ref.1, s32[1]{0:T(128)S(6)} %copy.12.count_ref, bf16[128,256]{1,0:T(8,128)(2,1)} %x_hbm.1, bf16[16,128,128]{2,1,0:T(8,128)(2,1)} %tiles_hbm.1, bf16[768,256]{1,0:T(8,128)(2,1)} %w_hbm.1, f32[1,256]{1,0:T(1,128)} %bitcast.1, ...), custom_call_target="tpu_custom_call" | custom-call | flops 2000000000 | bytes 4000000 | tf_op jit(solution)/shard_map/pallas_call | solution.py:368
  110.8 1.5 %copy.13 = bf16[128,256]{1,0:T(8,128)(2,1)} copy(bf16[128,256]{1,0:T(8,128)(2,1)} %get-tuple-element.4) | data formatting | bytes 131072
  112.2 2.1 %copy.14 = f32[768,256]{1,0:T(8,128)} copy(f32[768,256]{1,0:T(8,128)} %get-tuple-element.5) | data formatting | bytes 1572864
